TPU v7x, 32 devices: a whole 2x2x4 slice. The times are simulated.
32 devices in a mesh: space: 16 (over z, y, core), chan: 2 (over x).
Axes of the slice: x: 2, y: 2, z: 4, core: 2. Of those that a mesh axis runs over, the one named last changes fastest.
Arguments:
- activations: bfloat16 [256, 16, 4096], P('chan', 'space'), may hold values from -6 to 6
- filters: bfloat16 [256, 27, 256], P('chan'), may hold values from -0.078125 to 0.078125
- cotangent: bfloat16 [256, 16, 4096], P('chan', 'space'), may hold values from -6 to 6
Outputs:
- output: bfloat16 [256, 16, 4096], P('chan', 'space')
- input_grad: bfloat16 [256, 16, 4096], P('chan', 'space')
- filter_grad: float32 [256, 27, 256], P('chan')
All inputs are finite; a program needn't handle non-finite values.
Results may differ from a plain program's by a relative error of at most 0.001.
Values may be sent and summed in bfloat16 or wider, within the bound.
A program may use at most 192 MiB of HBM per device.

v0:
```python
import math

import jax
import jax.numpy as jnp
from jax import lax
from jax.sharding import PartitionSpec as P

HGT = 64
WID = 64


tap_offsets = tuple(
    (
        (depth_step, row_step, col_step)
        for depth_step in (-1, 0, 1)
        for row_step in (-1, 0, 1)
        for col_step in (-1, 0, 1)
    )
)


def with_halo(cells, sides, width):
    for axis, dim in sides:
        count = lax.axis_size(axis)
        ends = count - 1
        head = lax.slice_in_dim(cells, 0, width, axis=dim)
        tail = lax.slice_in_dim(cells, cells.shape[dim] - width, cells.shape[dim], axis=dim)
        cells = jnp.concatenate(
            [
                lax.ppermute(tail, axis, [(i, (i + 1) % count) for i in range(ends)]),
                cells,
                lax.ppermute(head, axis, [((i + 1) % count, i) for i in range(ends)]),
            ],
            axis=dim,
        )
    return cells


def plane_mask(row_step, col_step, slab_depth):
    position = jnp.arange(slab_depth * HGT * WID, dtype=jnp.int32)
    row_index = position // WID % HGT
    col_index = position % WID
    valid = (
        (row_index + row_step >= 0)
        & (row_index + row_step < HGT)
        & (col_index + col_step >= 0)
        & (col_index + col_step < WID)
    )
    return valid.astype(jnp.bfloat16)


def flatten_padded(padded):
    channels = padded.shape[0]
    flattened = padded.reshape(channels, -1)
    return jnp.pad(flattened, ((0, 0), (WID + 1, WID + 1)))


def shifted(flattened, depth_step, row_step, col_step, slab_depth):
    plane = HGT * WID
    begin = WID + 1 + plane + depth_step * plane + row_step * WID + col_step
    window = lax.slice_in_dim(flattened, begin, begin + slab_depth * plane, axis=1)
    return window * plane_mask(row_step, col_step, slab_depth)


def per_device(activations, filters, cotangent):
    slab_depth = activations.shape[1]
    plane = activations.shape[2]
    cells = slab_depth * plane
    filter_count = filters.shape[0]
    channel_count = activations.shape[0]
    padded_input = with_halo(activations, (("space", 1),), 1)
    padded_grad = with_halo(cotangent, (("space", 1),), 1)
    grad_cells = cotangent.reshape(filter_count, cells)
    empty_out = jnp.zeros((filter_count, cells), jnp.float32)
    out_total = empty_out
    flattened = flatten_padded(lax.all_gather(padded_input, "chan", axis=0, tiled=True))
    blocks = []
    for tap, forward_offset in enumerate(tap_offsets):
        moved = shifted(
            flattened, forward_offset[0], forward_offset[1], forward_offset[2], slab_depth
        )
        weights_tap = filters[:, tap, :]
        out_total = out_total + jnp.dot(weights_tap, moved, preferred_element_type=jnp.float32)
        blocks.append(
            lax.dot_general(
                grad_cells, moved, (((1,), (1,)), ((), ())), preferred_element_type=jnp.float32
            )
        )
    block = jnp.stack(blocks, axis=1)
    weight_total = block
    out_total, weight_total = (out_total, weight_total)
    scale = 1.0 / math.sqrt(slab_depth * lax.axis_size("space") * plane)
    filter_grad = lax.psum(weight_total, "space") * scale
    grad_flat = flatten_padded(padded_grad)
    tap_stack = jnp.concatenate(
        [
            shifted(grad_flat, -offset[0], -offset[1], -offset[2], slab_depth)
            for offset in tap_offsets
        ],
        axis=0,
    )
    weight_matrix = filters.transpose(2, 1, 0).reshape(filters.shape[2], -1)
    input_grad = lax.psum_scatter(
        jnp.dot(weight_matrix, tap_stack, preferred_element_type=jnp.float32).reshape(
            lax.axis_size("chan") * channel_count, slab_depth, plane
        ),
        "chan",
        scatter_dimension=0,
        tiled=True,
    ).astype(jnp.bfloat16)
    output = out_total.reshape(filter_count, slab_depth, plane).astype(jnp.bfloat16)
    return (output, input_grad, filter_grad)


def solution(mesh):
    in_specs = (P("chan", "space", None), P("chan", None, None), P("chan", "space", None))
    out_specs = (P("chan", "space", None), P("chan", "space", None), P("chan", None, None))
    return jax.shard_map(
        per_device, mesh=mesh, in_specs=in_specs, out_specs=out_specs, check_vma=False
    )
```

profile of v0, /device:TPU:0, one launch (start us, length us, event | category | flops | bytes accessed | tf_op | source)
XLA Modules:
  0.0 397.0 jit_solution(11063328750060638763)
XLA Ops:
  8.9 2.4 collective-permute-start.2
  14.0 5.2 %collective-permute-start = (bf16[128,1,4096]{0,2,1:T(8,128)(2,1)}, bf16[128,1,4096]{0,2,1:T(8,128)(2,1)S(1)}, u32[]{:S(2)}, u32[]{:S(2)}) collective-permute-start(bf16[128,1,4096]{0,2,1:T(8,128)(2,1)} %copy.9), channel_id=1, source_target_pairs={{0,2},{2,4},{4,6},{6,8},{8,10},{10,12},{12,14},{14,16},{16,18},{18... | collective-permute-start | bytes 3145736 | tf_op jit(solution)/shard_map/ppermute | solution.py:30
  21.6 2.2 pad_maximum_fusion.1
  41.9 9.3 %copy-done.7 = bf16[3456,4096]{0,1:T(8,128)(2,1)} copy-done((bf16[3456,4096]{0,1:T(8,128)(2,1)}, bf16[3456,4096]{0,1:T(8,128)(2,1)S(1)}, u32[]{:S(2)}) %copy-start.7) | copy-done | bytes 28311576
  51.2 3.2 pad_maximum_fusion
  65.5 98.1 %all-gather.2.cloned.1.call-done = bf16[256,3,4096]{0,2,1:T(8,128)(2,1)} async-done(((bf16[128,3,4096]{0,2,1:T(8,128)(2,1)}), bf16[256,3,4096]{0,2,1:T(8,128)(2,1)}) %all-gather.2.cloned.1.call-update) | async-done | bytes 6291472 | tf_op jit(solution)/shard_map/all_gather | solution.py:76
  163.6 4.1 %fusion.94 = f32[128,27,256]{0,2,1:T(8,128)} fusion(bf16[128,1,4096]{2,0,1:T(8,128)(2,1)} %param.5, bf16[4096]{0:T(1024)(128)(2,1)S(1)} %and_convert_fusion.8, bf16[256,12288]{0,1:T(8,128)(2,1)} %bitcast.357), kind=kOutput, calls=%fused_computation.151 | convolution fusion | flops 272629760 | bytes 7479296 | tf_op jit(solution)/shard_map/dot_general | solution.py:85
  169.8 2.2 fusion.90
  172.1 2.2 fusion.88
  176.4 2.2 fusion.76
  178.6 2.2 fusion.74
  182.9 2.2 fusion.70
  185.1 2.7 fusion.68
  189.9 2.2 fusion.64
  192.2 2.2 fusion.62
  196.5 2.2 fusion.58
  198.7 2.2 fusion.56
  203.0 2.2 fusion.52
  205.2 2.2 fusion.50
  207.4 2.3 fusion.48
  209.7 2.2 fusion.46
  211.9 2.2 fusion.44
  216.2 2.3 fusion.86
  218.5 2.3 fusion.84
  220.8 2.1 fusion.82
  222.9 2.3 fusion.80
  226.9 15.4 %convolution_bitcast_fusion = f32[256,1,4096]{0,2,1:T(8,128)} fusion(bf16[3456,4096]{0,1:T(8,128)(2,1)} %multiply_dynamic-update-slice_fusion, bf16[256,3456]{0,1:T(8,128)(2,1)S(1)} %bitcast.440), kind=kOutput, calls=%fused_computation | convolution fusion | flops 7247757312 | bytes 34275328 | tf_op jit(solution)/shard_map/dot_general | solution.py:104
  242.3 2.7 fusion.14
  271.1 60.4 %all-reduce.4.cloned.1.call-done = f32[128,27,256]{0,2,1:T(8,128)} async-done(((f32[128,27,256]{0,2,1:T(8,128)}), f32[128,27,256]{0,2,1:T(8,128)}) %all-reduce.4.cloned.1.call-update) | async-done | bytes 3538960 | tf_op jit(solution)/shard_map/psum | solution.py:93
  331.6 2.3 broadcast_multiply_fusion
  333.8 2.9 copy.17
  336.8 50.3 %reduce-scatter.2.cloned.1.call-done = f32[128,1,4096]{0,2,1:T(8,128)} async-done(((f32[256,1,4096]{0,2,1:T(8,128)}), f32[128,1,4096]{0,2,1:T(8,128)}) %reduce-scatter.2.cloned.1.call-update) | async-done | bytes 2097168 | tf_op jit(solution)/shard_map/reduce_scatter | solution.py:103
  (106 shorter events, 81.1 us)
Async XLA Ops:
  7.2 5.5 %copy-start.5 = (bf16[128,1,4096]{2,0,1:T(8,128)(2,1)S(1)}, bf16[128,1,4096]{2,0,1:T(8,128)(2,1)}, u32[]{:S(2)}) copy-start(bf16[128,1,4096]{2,0,1:T(8,128)(2,1)} %param.3) | copy-start | bytes 3145732
  7.2 156.4 %all-gather.2.cloned.1.call-start = ((), (), s32[]{:S(2)}) async-start(), calls=%async_computation.1 | async-start | bytes 9437184 | tf_op jit(solution)/shard_map/all_gather | solution.py:76
  8.9 11.7 %copy-start.2 = (bf16[128,1,4096]{0,2,1:T(8,128)(2,1)}, bf16[128,1,4096]{0,2,1:T(8,128)(2,1)S(1)}, u32[]{:S(2)}) copy-start(bf16[128,1,4096]{0,2,1:T(8,128)(2,1)S(1)} %copy.12) | copy-start | bytes 3145732
  8.9 11.7 %collective-permute-start.2 = (bf16[128,1,4096]{0,2,1:T(8,128)(2,1)S(1)}, bf16[128,1,4096]{0,2,1:T(8,128)(2,1)S(1)}, u32[]{:S(2)}, u32[]{:S(2)}) collective-permute-start(bf16[128,1,4096]{0,2,1:T(8,128)(2,1)S(1)} %copy.12), channel_id=1, source_target_pairs={{0,2},{2,4},{4,6},{6,8},{8,10},{10,12},{12,14},{14,16},{16,18},{18... | collective-permute-start | bytes 3145736 | tf_op jit(solution)/shard_map/ppermute | solution.py:30
  11.4 10.2 %collective-permute-start.3 = (bf16[128,1,4096]{0,2,1:T(8,128)(2,1)S(1)}, bf16[128,1,4096]{0,2,1:T(8,128)(2,1)}, u32[]{:S(2)}, u32[]{:S(2)}) collective-permute-start(bf16[128,1,4096]{0,2,1:T(8,128)(2,1)S(1)} %copy.12), channel_id=1, source_target_pairs={{2,0},{4,2},{6,4},{8,6},{10,8},{12,10},{14,12},{16,14},{18,16},{20... | collective-permute-start | bytes 3145736 | tf_op jit(solution)/shard_map/ppermute | solution.py:32
  14.0 27.9 %collective-permute-start = (bf16[128,1,4096]{0,2,1:T(8,128)(2,1)}, bf16[128,1,4096]{0,2,1:T(8,128)(2,1)S(1)}, u32[]{:S(2)}, u32[]{:S(2)}) collective-permute-start(bf16[128,1,4096]{0,2,1:T(8,128)(2,1)} %copy.9), channel_id=1, source_target_pairs={{0,2},{2,4},{4,6},{6,8},{8,10},{10,12},{12,14},{14,16},{16,18},{18... | collective-permute-start | bytes 3145736 | tf_op jit(solution)/shard_map/ppermute | solution.py:30
  19.1 22.7 %collective-permute-start.1 = (bf16[128,1,4096]{0,2,1:T(8,128)(2,1)}, bf16[128,1,4096]{0,2,1:T(8,128)(2,1)S(1)}, u32[]{:S(2)}, u32[]{:S(2)}) collective-permute-start(bf16[128,1,4096]{0,2,1:T(8,128)(2,1)} %copy.9), channel_id=1, source_target_pairs={{2,0},{4,2},{6,4},{8,6},{10,8},{12,10},{14,12},{16,14},{18,16},{20... | collective-permute-start | bytes 3145736 | tf_op jit(solution)/shard_map/ppermute | solution.py:32
  20.6 1.0 copy-start.6
  41.9 9.3 %copy-start.7 = (bf16[3456,4096]{0,1:T(8,128)(2,1)}, bf16[3456,4096]{0,1:T(8,128)(2,1)S(1)}, u32[]{:S(2)}) copy-start(bf16[3456,4096]{0,1:T(8,128)(2,1)S(1)} %fusion.99) | copy-start | bytes 84934656
  54.5 277.1 %all-reduce.4.cloned.1.call-start = ((), (), s32[]{:S(2)}) async-start(), calls=%async_computation.3 | async-start | bytes 7077888 | tf_op jit(solution)/shard_map/psum | solution.py:93
  163.6 4.1 %copy-start = (bf16[256,3,4096]{0,2,1:T(8,128)(2,1)S(1)}, bf16[256,3,4096]{0,2,1:T(8,128)(2,1)}, u32[]{:S(2)}) copy-start(bf16[256,3,4096]{0,2,1:T(8,128)(2,1)} %all-gather.2.cloned.1.call-done) | copy-start | bytes 18874372
  163.6 4.1 %copy-start.1 = (bf16[128,1,4096]{2,0,1:T(8,128)(2,1)S(1)}, bf16[128,1,4096]{2,0,1:T(8,128)(2,1)}, u32[]{:S(2)}) copy-start(bf16[128,1,4096]{2,0,1:T(8,128)(2,1)} %param.5) | copy-start | bytes 3145732
  225.2 161.9 %reduce-scatter.2.cloned.1.call-start = ((), (), s32[]{:S(2)}) async-start(), calls=%async_computation.2 | async-start | bytes 6291456 | tf_op jit(solution)/shard_map/reduce_scatter | solution.py:103
  225.2 1.7 copy-start.3
  242.3 2.8 slice-start
  242.3 3.6 slice-start.1
  242.3 4.1 %copy-start.4 = (bf16[128,27,256]{2,0,1:T(8,128)(2,1)S(1)}, bf16[128,27,256]{2,0,1:T(8,128)(2,1)}, u32[]{:S(2)}) copy-start(bf16[128,27,256]{2,0,1:T(8,128)(2,1)} %param.4) | copy-start | bytes 5308420
Sparse Core Ops, SparseCore 0:
  54.6 108.9 all-gather.1
  225.3 106.2 all-reduce.3
  333.9 53.1 reduce-scatter.1
where the time goes:
time: 405 us; the launch traced here: 397 us
  waiting for transfers between devices  209 us (52%)
  matrix products  103 us (25%)
  other arithmetic  40 us (10%)
  local copies, waits for them, and re-layouts  20.3 us (5%)
  between operations  14.7 us (4%)
  starting transfers between devices  10.3 us (3%)
    all_gather x1, waiting for transfers between devices, per_device(): lax.all_gather(padded_input, 'chan', axis=0, tiled=True)  98.1 us
    dot_general x27, matrix products, per_device(): lax.dot_general(grad_cells, moved, (((1,), (1,)), ((), ())), preferred_el...  61.6 us
    psum x1, waiting for transfers between devices, per_device(): filter_grad = lax.psum(weight_total, 'space') * scale  60.4 us
    reduce_scatter x1, waiting for transfers between devices, per_device(): lax.psum_scatter(jnp.dot(weight_matrix, tap_stack, preferred_element_type...  50.3 us
    unnamed x27, other arithmetic  28.9 us
    dot_general x27, matrix products, per_device(): jnp.dot(weights_tap, moved, preferred_element_type=jnp.float32)  25.9 us
    unnamed x25, local copies, waits for them, and re-layouts  20.3 us
    dot_general x1, matrix products, per_device(): jnp.dot(weight_matrix, tap_stack, preferred_element_type=jnp.float32)  15.4 us
  transfers between devices with their start and end apart: 7, of which 3 were waited for; matrix products, arithmetic and copies ran while one was open for 21% of the time, Pallas kernels for 0%

commit v1 on v0

v1 whole, which is shorter than its diff:
```python
import math

import jax
import jax.numpy as jnp
from jax import lax
from jax.experimental import pallas as pl
from jax.experimental.pallas import tpu as pltpu
from jax.sharding import PartitionSpec as P

HGT = 64
WID = 64


def swap(value, axis, bit):
    count = lax.axis_size(axis)
    return lax.ppermute(value, axis, [(i, i ^ (1 << bit)) for i in range(count)])


def outward(value, axis):
    count = lax.axis_size(axis)
    pairs = []
    for i in range(count):
        j = i + 1 if i % 2 else i - 1
        if 0 <= j < count:
            pairs.append((i, j))
    return lax.ppermute(value, axis, pairs)


def sum_over(value, axis, bits):
    me = lax.axis_index(axis)
    rows = value.shape[0]
    for bit in bits:
        half = rows // 2
        mine = (me >> bit) & 1
        keep = lax.dynamic_slice_in_dim(value, mine * half, half, 0)
        send = lax.dynamic_slice_in_dim(value, (1 - mine) * half, half, 0)
        value = keep + swap(send, axis, bit)
        rows = half
    for bit in reversed(bits):
        mine = (me >> bit) & 1
        other = swap(value, axis, bit)
        low = jnp.where(mine == 0, value, other)
        high = jnp.where(mine == 0, other, value)
        value = jnp.concatenate([low, high], axis=0)
    return value


def fill_taps(cells, taps):
    count, plane = cells.shape
    tile = 128
    wide = cells.astype(jnp.float32)
    lane = lax.broadcasted_iota(jnp.int32, (count, plane), 1)
    col = lane % WID
    first = lax.broadcasted_iota(jnp.int32, (count, tile), 1) < WID
    for at, step in enumerate((-1, 0, 1)):
        if step == 0:
            moved = wide
        else:
            ok = col > 0 if step == -1 else col < WID - 1
            moved = jnp.where(ok, pltpu.roll(wide, (-step) % plane, 1), 0.0)
        turned = pltpu.roll(moved, WID, 1)
        kind = taps.dtype
        low = turned[:, :tile]
        taps[pl.ds((3 + at) * count, count), :] = moved.astype(kind)
        up = pl.ds(at * count, count)
        taps[up, 0:tile] = jnp.where(first, 0.0, low).astype(kind)
        taps[up, tile:plane] = turned[:, tile:].astype(kind)
        down = pl.ds((6 + at) * count, count)
        taps[down, 0 : plane - tile] = turned[:, tile:].astype(kind)
        taps[down, plane - tile : plane] = jnp.where(first, low, 0.0).astype(kind)


def conv_kernel(width, volume, weights, out, taps, total):
    depth = pl.program_id(0)
    fill_taps(volume[0], taps)

    @pl.loop(0, out.shape[1] // width)
    def _(i):
        at = pl.ds(pl.multiple_of(i * width, width), width)
        part = jnp.dot(weights[0], taps[:, at], preferred_element_type=jnp.float32)

        @pl.when(depth == 0)
        def _():
            total[:, at] = part

        @pl.when(depth > 0)
        def _():
            total[:, at] += part

        @pl.when(depth == 2)
        def _():
            out[:, at] = total[:, at].astype(out.dtype)


def conv(volume, weights, kind):
    _, count, plane = volume.shape
    rows = weights.shape[1]
    return pl.pallas_call(
        lambda *refs: conv_kernel(512, *refs),
        grid=(3,),
        in_specs=[
            pl.BlockSpec((1, count, plane), lambda a: (a, 0, 0)),
            pl.BlockSpec((1, rows, 9 * count), lambda a: (a, 0, 0)),
        ],
        out_specs=pl.BlockSpec((rows, plane), lambda a: (0, 0)),
        out_shape=jax.ShapeDtypeStruct((rows, plane), kind),
        scratch_shapes=[
            pltpu.VMEM((9 * count, plane), jnp.bfloat16),
            pltpu.VMEM((rows, plane), jnp.float32),
        ],
        compiler_params=pltpu.CompilerParams(vmem_limit_bytes=50 << 20),
        cost_estimate=pl.CostEstimate(
            flops=2 * rows * 27 * count * plane,
            bytes_accessed=3 * count * plane * 2 + rows * plane * 4,
            transcendentals=0,
        ),
    )(volume, weights)


def grad_kernel(scale, width, volume, other, out, taps):
    fill_taps(volume[0], taps)
    out[...] = jnp.zeros_like(out)

    @pl.loop(0, other.shape[0] // width)
    def _(i):
        at = pl.ds(pl.multiple_of(i * width, width), width)
        out[0] += jnp.dot(taps[:, at], other[at, :], preferred_element_type=jnp.float32)

    out[...] = out[...] * scale


def kernel_grad(volume, other, scale):
    _, count, plane = volume.shape
    columns = other.shape[1]
    return pl.pallas_call(
        lambda *refs: grad_kernel(scale, 1024, *refs),
        grid=(3,),
        in_specs=[
            pl.BlockSpec((1, count, plane), lambda a: (a, 0, 0)),
            pl.BlockSpec((plane, columns), lambda a: (0, 0)),
        ],
        out_specs=pl.BlockSpec((1, 9 * count, columns), lambda a: (a, 0, 0)),
        out_shape=jax.ShapeDtypeStruct((3, 9 * count, columns), jnp.float32),
        scratch_shapes=[pltpu.VMEM((9 * count, plane), jnp.bfloat16)],
        compiler_params=pltpu.CompilerParams(vmem_limit_bytes=50 << 20),
        cost_estimate=pl.CostEstimate(
            flops=2 * columns * 27 * count * plane,
            bytes_accessed=3 * count * plane * 2 + 27 * count * columns * 4,
            transcendentals=0,
        ),
    )(volume, other)


def per_device(activations, filters, cotangent):
    channels, _, plane = activations.shape
    filter_count, taps, all_channels = filters.shape
    space = lax.axis_size("space")
    me = lax.axis_index("space")
    side = lax.axis_index("chan")
    odd = me % 2
    act = activations[:, 0, :]
    cot = cotangent[:, 0, :]

    def chan_swap(value):
        return lax.ppermute(value, "chan", [(0, 1), (1, 0)])

    def by_channel(own, peer):
        return jnp.where(side == 0, jnp.concatenate([own, peer], 0), jnp.concatenate([peer, own], 0))

    def by_depth(own, inner, outer):
        low = jnp.where(odd == 0, outer, inner)
        high = jnp.where(odd == 0, inner, outer)
        return jnp.stack([low, own, high], axis=0)

    cot_in = swap(cot, "space", 0)
    cot_out = outward(cot, "space")
    act_own = by_channel(act, chan_swap(act))
    cot_volume, act_late, act_own_late = lax.optimization_barrier(
        (by_depth(cot, cot_in, cot_out), act, act_own)
    )
    act_out = outward(act_late, "space")
    act_in = swap(act_own_late, "space", 0)

    scale = 1.0 / math.sqrt(space * plane)
    grad = kernel_grad(cot_volume, act_own.T, scale).reshape(-1, all_channels)
    bits = list(range(space.bit_length() - 1))
    half = all_channels // 2
    first = sum_over(grad[:, :half], "space", bits)
    second = sum_over(grad[:, half:], "space", bits[:1] + bits[2:] + bits[1:2])
    filter_grad = jnp.concatenate([first, second], axis=1).reshape(taps, filter_count, all_channels)
    filter_grad = filter_grad[::-1].transpose(1, 0, 2)

    turned = filters[:, ::-1, :].transpose(2, 1, 0)
    turned = jnp.where(
        side == 0,
        jnp.concatenate([turned[channels:], turned[:channels]], 0),
        turned,
    )
    turned = turned.reshape(all_channels, 3, 9 * filter_count).transpose(1, 0, 2)
    partial = conv(cot_volume, turned, jnp.float32)
    input_grad = partial[channels:] + chan_swap(partial[:channels])
    input_grad = input_grad.astype(jnp.bfloat16).reshape(channels, 1, plane)

    act_volume = by_depth(act_own, act_in, by_channel(act_out, chan_swap(act_out)))
    straight = filters.reshape(filter_count, 3, 9 * all_channels).transpose(1, 0, 2)
    output = conv(act_volume, straight, jnp.bfloat16).reshape(filter_count, 1, plane)
    return (output, input_grad, filter_grad)


def solution(mesh):
    in_specs = (P("chan", "space", None), P("chan", None, None), P("chan", "space", None))
    out_specs = (P("chan", "space", None), P("chan", "space", None), P("chan", None, None))
    return jax.shard_map(
        per_device, mesh=mesh, in_specs=in_specs, out_specs=out_specs, check_vma=False
    )
```

time: 405 us -> 211 us (0.52); the launches traced: 397 us -> 211 us
  waiting for transfers between devices: 209 us -> 56.2 us
  matrix products: 103 us -> 0 us
  Pallas kernels: 0 us -> 70.6 us
  starting transfers between devices: 10.3 us -> 36.7 us
  other arithmetic: 40 us -> 20.6 us
  between operations: 14.7 us -> 1.02 us
  local copies, waits for them, and re-layouts: 20.3 us -> 25.6 us
    dot_general x55 -> x0, matrix products: 103 us -> none  [the longest x27 61.6 us: per_device(): lax.dot_general(grad_cells, moved, (((1,), (1,)), ((), ())), preferred_el...]
    all_gather x1 -> x0, waiting for transfers between devices: 98.1 us -> none  [per_device(): lax.all_gather(padded_input, 'chan', axis=0, tiled=True)]
    pallas_call x0 -> x3, Pallas kernels: none -> 70.6 us  [the longest x2 52.2 us: conv(): pl.pallas_call(lambda *refs: conv_kernel(512, *refs), grid=(3,), in_specs...]
    psum x1 -> x0, waiting for transfers between devices: 60.4 us -> none  [per_device(): filter_grad = lax.psum(weight_total, 'space') * scale]
    ppermute x4 -> x23, waiting for transfers between devices: 0.01 us -> 56.2 us  [the longest x18 46.2 us: swap(): return lax.ppermute(value, axis, [(i, i ^ 1 << bit) for i in range(count)])]
    reduce_scatter x1 -> x0, waiting for transfers between devices: 50.3 us -> none  [per_device(): lax.psum_scatter(jnp.dot(weight_matrix, tap_stack, preferred_element_type...]
    unnamed x27 -> x0, other arithmetic: 28.9 us -> none
    ppermute x4 -> x23, starting transfers between devices: 10.2 us -> 36.7 us  [the longest x18 30.4 us: swap(): return lax.ppermute(value, axis, [(i, i ^ 1 << bit) for i in range(count)])]
  transfers between devices with their start and end apart: 7 -> 23, of which waited for: 3 -> 9; matrix products, arithmetic and copies ran while one was open for 21% -> 18% of each run, Pallas kernels for 0% -> 25%
where the time goes in v1:
time: 211 us
  Pallas kernels  70.6 us (33%)
  waiting for transfers between devices  56.2 us (27%)
  starting transfers between devices  36.7 us (17%)
  local copies, waits for them, and re-layouts  25.6 us (12%)
  other arithmetic  20.6 us (10%)
    pallas_call x2, Pallas kernels, conv(): pl.pallas_call(lambda *refs: conv_kernel(512, *refs), grid=(3,), in_specs...  52.2 us
    ppermute x18, waiting for transfers between devices, swap(): return lax.ppermute(value, axis, [(i, i ^ 1 << bit) for i in range(count)])  46.2 us
    ppermute x18, starting transfers between devices, swap(): return lax.ppermute(value, axis, [(i, i ^ 1 << bit) for i in range(count)])  30.4 us
    pallas_call x1, Pallas kernels, kernel_grad(): pl.pallas_call(lambda *refs: grad_kernel(scale, 1024, *refs), grid=(3,),...  18.4 us
    ppermute x3, waiting for transfers between devices, chan_swap(): return lax.ppermute(value, 'chan', [(0, 1), (1, 0)])  9.98 us
    another operation x1, local copies, waits for them, and re-layouts, by_depth(): return jnp.stack([low, own, high], axis=0)  8.68 us
    another operation x4, other arithmetic, by_depth(): return jnp.stack([low, own, high], axis=0)  8.21 us
    select_n x2, other arithmetic, by_channel(): jnp.where(side == 0, jnp.concatenate([own, peer], 0), jnp.concatenate([pe...  5.9 us
  transfers between devices with their start and end apart: 23, of which 9 were waited for; matrix products, arithmetic and copies ran while one was open for 18% of the time, Pallas kernels for 25%

profile of v1, /device:TPU:0, one launch (start us, length us, event | category | flops | bytes accessed | tf_op | source)
XLA Modules:
  0.0 210.7 jit_solution(81732136541058216)
XLA Ops:
  0.6 1.8 collective-permute-start
  2.4 3.4 %collective-permute-start.1 = (bf16[128,4096]{1,0:T(8,128)(2,1)}, bf16[128,4096]{1,0:T(8,128)(2,1)}, u32[]{:S(2)}, u32[]{:S(2)}) collective-permute-start(bf16[128,4096]{1,0:T(8,128)(2,1)} %bitcast.37), channel_id=1, source_target_pairs={{0,2},{2,0},{4,6},{6,4},{8,10},{10,8},{12,14},{14,12},{16,18},{18,... | collective-permute-start | bytes 3145736 | tf_op jit(solution)/shard_map/ppermute | solution.py:16
  5.8 2.3 %copy.9 = bf16[128,1,4096]{0,2,1:T(8,128)(2,1)} copy(bf16[128,1,4096]{2,0,1:T(8,128)(2,1)} %param.3) | data formatting | bytes 2097152 | tf_op args[0]
  9.6 2.2 %copy.11 = bf16[128,27,256]{0,2,1:T(8,128)(2,1)} copy(bf16[128,27,256]{2,0,1:T(8,128)(2,1)S(1)} %copy-done) | data formatting | bytes 3538944 | tf_op args[1]
  12.4 1.9 maximum_select_fusion.3
  14.3 2.7 %copy.14 = bf16[256,3,1152]{2,0,1:T(8,128)(2,1)S(1)} copy(bf16[256,3,1152]{0,2,1:T(8,128)(2,1)} %bitcast.34) | data formatting | bytes 3538944 | tf_op jit(solution)/shard_map/reshape | solution.py:199
  17.0 2.6 %copy.12 = bf16[128,3,2304]{2,0,1:T(8,128)(2,1)S(1)} copy(bf16[128,3,2304]{0,2,1:T(8,128)(2,1)} %bitcast.33) | data formatting | bytes 3538944 | tf_op jit(solution)/shard_map/reshape | solution.py:205
  19.7 1.8 select_bitcast_fusion.3
  21.5 2.0 pad_maximum_fusion.1.refs_0_
  23.5 10.0 %collective-permute-done.2 = bf16[128,4096]{0,1:T(8,128)(2,1)} collective-permute-done((bf16[128,4096]{0,1:T(8,128)(2,1)}, bf16[128,4096]{0,1:T(8,128)(2,1)}, u32[]{:S(2)}, u32[]{:S(2)}) %collective-permute-start.2) | collective-permute-done | bytes 1048608 | tf_op jit(solution)/shard_map/ppermute | solution.py:165
  33.5 3.0 %maximum_select_fusion = bf16[256,4096]{0,1:T(8,128)(2,1)S(1)} fusion(bf16[128,4096]{0,1:T(8,128)(2,1)} %collective-permute-done.2, bf16[128,4096]{0,1:T(8,128)(2,1)} %bitcast.4, pred[]{:T(512)S(6)} %eq.15), kind=kLoop, calls=%fused_computation.6 | loop fusion | flops 9437184 | bytes 4194305 | tf_op jit(solution)/shard_map/jit(_where)/select_n | solution.py:168
  36.5 18.4 %shard_map.60 = f32[3,1152,256]{2,1,0:T(8,128)} custom-call(bf16[3,128,4096]{2,1,0:T(8,128)(2,1)} %pad_maximum_fusion.1.refs_0_, bf16[4096,256]{1,0:T(8,128)(2,1)S(1)} %bitcast.29), custom_call_target="tpu_custom_call" | custom-call | flops 7247757312 | bytes 6684672 | tf_op jit(solution)/shard_map/pallas_call | solution.py:135
  54.9 2.2 %fusion.2 = (f32[3456,128]{1,0:T(8,128)S(1)}, f32[3456,128]{1,0:T(8,128)S(1)}) fusion(f32[3456,256]{1,0:T(8,128)} %bitcast.35), kind=kLoop, calls=%fused_computation.54 | loop fusion | bytes 7077888 | tf_op jit(solution)/shard_map/slice | solution.py:188
  57.9 23.2 %shard_map.59 = f32[256,4096]{1,0:T(8,128)} custom-call(bf16[3,128,4096]{2,1,0:T(8,128)(2,1)} %pad_maximum_fusion.1.refs_0_, bf16[3,256,1152]{2,1,0:T(8,128)(2,1)S(1)} %bitcast.31), custom_call_target="tpu_custom_call" | custom-call | flops 7247757312 | bytes 7340032 | tf_op jit(solution)/shard_map/pallas_call | solution.py:98
  81.1 1.7 slice.27
  85.3 3.0 %collective-permute-start.5 = (bf16[256,4096]{0,1:T(8,128)(2,1)S(1)}, bf16[256,4096]{0,1:T(8,128)(2,1)S(1)}, u32[]{:S(2)}, u32[]{:S(2)}) collective-permute-start(bf16[256,4096]{0,1:T(8,128)(2,1)S(1)} %maximum_select_fusion), channel_id=1, source_target_pairs={{0,2},{2,0},{4,6},{6,4},{8,10},{10,8},{12,14},{14,12},{16,18},{18,... | collective-permute-start | bytes 6291464 | tf_op jit(solution)/shard_map/ppermute | solution.py:16
  91.7 2.9 %maximum_select_fusion.2 = bf16[1,256,4096]{1,2,0:T(8,128)(2,1)S(1)} fusion(bf16[1,128,4096]{1,2,0:T(8,128)(2,1)} %bitcast.7, bf16[1,128,4096]{1,2,0:T(8,128)(2,1)} %bitcast.6, pred[]{:T(512)S(6)} %eq.15), kind=kLoop, calls=%fused_computation.8 | loop fusion | flops 9437184 | bytes 4194305 | tf_op jit(solution)/shard_map/jit(_where)/select_n | solution.py:168
  95.2 15.1 %collective-permute-done.8 = f32[864,128]{1,0:T(8,128)S(1)} collective-permute-done((f32[864,128]{1,0:T(8,128)S(1)}, f32[864,128]{1,0:T(8,128)S(1)}, u32[]{:S(2)}, u32[]{:S(2)}) %collective-permute-start.8) | collective-permute-done | bytes 442400 | tf_op jit(solution)/shard_map/ppermute | solution.py:16
  110.4 12.9 %collective-permute-start.9 = (f32[432,128]{1,0:T(8,128)S(1)}, f32[432,128]{1,0:T(8,128)S(1)}, u32[]{:S(2)}, u32[]{:S(2)}) collective-permute-start(f32[432,128]{1,0:T(8,128)S(1)} %constant_dynamic-slice_fusion.5), channel_id=1, source_target_pairs={{0,8},{2,10},{4,12},{6,14},{8,0},{10,2},{12,4},{14,6},{16,24},{18,... | collective-permute-start | bytes 663560 | tf_op jit(solution)/shard_map/ppermute | solution.py:16
  123.4 2.7 %collective-permute-start.17 = (f32[432,128]{1,0:T(8,128)S(1)}, f32[432,128]{1,0:T(8,128)S(1)}, u32[]{:S(2)}, u32[]{:S(2)}) collective-permute-start(f32[432,128]{1,0:T(8,128)S(1)} %constant_dynamic-slice_fusion.1), channel_id=1, source_target_pairs={{0,16},{2,18},{4,20},{6,22},{8,24},{10,26},{12,28},{14,30},{16,0},... | collective-permute-start | bytes 663560 | tf_op jit(solution)/shard_map/ppermute | solution.py:16
  126.0 6.6 %collective-permute-done.9 = f32[432,128]{1,0:T(8,128)S(1)} collective-permute-done((f32[432,128]{1,0:T(8,128)S(1)}, f32[432,128]{1,0:T(8,128)S(1)}, u32[]{:S(2)}, u32[]{:S(2)}) %collective-permute-start.9) | collective-permute-done | bytes 221216 | tf_op jit(solution)/shard_map/ppermute | solution.py:16
  132.8 5.0 %collective-permute-done.17 = f32[432,128]{1,0:T(8,128)S(1)} collective-permute-done((f32[432,128]{1,0:T(8,128)S(1)}, f32[432,128]{1,0:T(8,128)S(1)}, u32[]{:S(2)}, u32[]{:S(2)}) %collective-permute-start.17) | collective-permute-done | bytes 221216 | tf_op jit(solution)/shard_map/ppermute | solution.py:16
  138.0 2.0 collective-permute-done.10
  140.1 3.2 %collective-permute-done.18 = f32[216,128]{1,0:T(8,128)S(1)} collective-permute-done((f32[216,128]{1,0:T(8,128)S(1)}, f32[216,128]{1,0:T(8,128)S(1)}, u32[]{:S(2)}, u32[]{:S(2)}) %collective-permute-start.18) | collective-permute-done | bytes 110624 | tf_op jit(solution)/shard_map/ppermute | solution.py:16
  143.4 4.8 %collective-permute-done.11 = f32[216,128]{1,0:T(8,128)S(1)} collective-permute-done((f32[216,128]{1,0:T(8,128)S(1)}, f32[216,128]{1,0:T(8,128)S(1)}, u32[]{:S(2)}, u32[]{:S(2)}) %collective-permute-start.11) | collective-permute-done | bytes 110624 | tf_op jit(solution)/shard_map/ppermute | solution.py:16
  148.4 1.8 collective-permute-start.20
  150.2 8.7 %collective-permute-done.12 = f32[432,128]{1,0:T(8,128)S(1)} collective-permute-done((f32[432,128]{1,0:T(8,128)S(1)}, f32[432,128]{1,0:T(8,128)S(1)}, u32[]{:S(2)}, u32[]{:S(2)}) %collective-permute-start.12) | collective-permute-done | bytes 221216 | tf_op jit(solution)/shard_map/ppermute | solution.py:16
  159.0 1.7 collective-permute-start.13
  164.2 3.2 %pad_maximum_fusion = bf16[3,256,4096]{1,2,0:T(8,128)(2,1)} fusion(bf16[1,256,4096]{1,2,0:T(8,128)(2,1)S(1)} %get-tuple-element.10, bf16[1,256,4096]{1,2,0:T(8,128)(2,1)S(1)} %maximum_select_fusion.2, bf16[1,256,4096]{1,2,0:T(8,128)(2,1)S(1)} %get-tuple-element.9), kind=kLoop, calls=%fused_computation | loop fusion | flops 6291456 | bytes 12582912 | tf_op jit(solution)/shard_map/stack | solution.py:173
  167.4 8.7 %copy.13.refs_0_ = bf16[3,256,4096]{2,1,0:T(8,128)(2,1)} copy(bf16[3,256,4096]{1,2,0:T(8,128)(2,1)} %pad_maximum_fusion) | data formatting | bytes 12582912 | tf_op jit(solution)/shard_map/stack | solution.py:173
  179.0 29.0 %shard_map.58 = bf16[128,4096]{1,0:T(8,128)(2,1)} custom-call(bf16[3,256,4096]{2,1,0:T(8,128)(2,1)} %copy.13.refs_0_, bf16[3,128,2304]{2,1,0:T(8,128)(2,1)S(1)} %bitcast.30), custom_call_target="tpu_custom_call" | custom-call | flops 7247757312 | bytes 8388608 | tf_op jit(solution)/shard_map/pallas_call | solution.py:98
  208.5 2.2 %reverse_bitcast_fusion = f32[128,27,256]{2,0,1:T(8,128)} fusion(f32[27,128,256]{2,1,0:T(8,128)S(1)} %bitcast.32), kind=kLoop, calls=%fused_computation.2 | loop fusion | bytes 7077888 | tf_op jit(solution)/shard_map/transpose | solution.py:191
  (72 shorter events, 17.0 us)
Async XLA Ops:
  0.6 9.0 %copy-start = (bf16[128,27,256]{2,0,1:T(8,128)(2,1)S(1)}, bf16[128,27,256]{2,0,1:T(8,128)(2,1)}, u32[]{:S(2)}) copy-start(bf16[128,27,256]{2,0,1:T(8,128)(2,1)} %param.4) | copy-start | bytes 5308420
  0.6 19.0 %collective-permute-start = (bf16[128,4096]{1,0:T(8,128)(2,1)}, bf16[128,4096]{1,0:T(8,128)(2,1)}, u32[]{:S(2)}, u32[]{:S(2)}) collective-permute-start(bf16[128,4096]{1,0:T(8,128)(2,1)} %bitcast.36), channel_id=1, source_target_pairs={{2,4},{4,2},{6,8},{8,6},{10,12},{12,10},{14,16},{16,14},{18,20},{2... | collective-permute-start | bytes 3145736 | tf_op jit(solution)/shard_map/ppermute | solution.py:26
  2.4 17.3 %collective-permute-start.1 = (bf16[128,4096]{1,0:T(8,128)(2,1)}, bf16[128,4096]{1,0:T(8,128)(2,1)}, u32[]{:S(2)}, u32[]{:S(2)}) collective-permute-start(bf16[128,4096]{1,0:T(8,128)(2,1)} %bitcast.37), channel_id=1, source_target_pairs={{0,2},{2,0},{4,6},{6,4},{8,10},{10,8},{12,14},{14,12},{16,18},{18,... | collective-permute-start | bytes 3145736 | tf_op jit(solution)/shard_map/ppermute | solution.py:16
  8.1 25.4 %collective-permute-start.2 = (bf16[128,4096]{0,1:T(8,128)(2,1)}, bf16[128,4096]{0,1:T(8,128)(2,1)}, u32[]{:S(2)}, u32[]{:S(2)}) collective-permute-start(bf16[128,4096]{0,1:T(8,128)(2,1)} %bitcast.4), channel_id=1, source_target_pairs={{0,1},{1,0},{2,3},{3,2},{4,5},{5,4},{6,7},{7,6},{8,9},{9,8},{10,11... | collective-permute-start | bytes 3145736 | tf_op jit(solution)/shard_map/ppermute | solution.py:165
  19.7 1.9 copy-start.2
  57.2 31.1 %collective-permute-start.7 = (f32[1728,128]{1,0:T(8,128)S(1)}, f32[1728,128]{1,0:T(8,128)S(1)}, u32[]{:S(2)}, u32[]{:S(2)}) collective-permute-start(f32[1728,128]{1,0:T(8,128)S(1)} %constant_dynamic-slice_fusion.7), channel_id=1, source_target_pairs={{0,2},{2,0},{4,6},{6,4},{8,10},{10,8},{12,14},{14,12},{16,18},{18,... | collective-permute-start | bytes 2654216 | tf_op jit(solution)/shard_map/ppermute | solution.py:16
  57.3 32.5 %collective-permute-start.15 = (f32[1728,128]{1,0:T(8,128)S(1)}, f32[1728,128]{1,0:T(8,128)S(1)}, u32[]{:S(2)}, u32[]{:S(2)}) collective-permute-start(f32[1728,128]{1,0:T(8,128)S(1)} %constant_dynamic-slice_fusion.3), channel_id=1, source_target_pairs={{0,2},{2,0},{4,6},{6,4},{8,10},{10,8},{12,14},{14,12},{16,18},{18,... | collective-permute-start | bytes 2654216 | tf_op jit(solution)/shard_map/ppermute | solution.py:16
  82.8 78.8 %collective-permute-start.6 = (f32[128,4096]{1,0:T(8,128)S(1)}, f32[128,4096]{1,0:T(8,128)S(1)}, u32[]{:S(2)}, u32[]{:S(2)}) collective-permute-start(f32[128,4096]{1,0:T(8,128)S(1)} %slice.27), channel_id=1, source_target_pairs={{0,1},{1,0},{2,3},{3,2},{4,5},{5,4},{6,7},{7,6},{8,9},{9,8},{10,11... | collective-permute-start | bytes 6291464 | tf_op jit(solution)/shard_map/ppermute | solution.py:165
  84.4 10.3 %collective-permute-start.3 = (bf16[128,4096]{0,1:T(8,128)(2,1)}, bf16[128,4096]{0,1:T(8,128)(2,1)S(1)}, u32[]{:S(2)}, u32[]{:S(2)}) collective-permute-start(bf16[128,4096]{0,1:T(8,128)(2,1)} %bitcast.4), channel_id=1, source_target_pairs={{2,4},{4,2},{6,8},{8,6},{10,12},{12,10},{14,16},{16,14},{18,20},{2... | collective-permute-start | bytes 3145736 | tf_op jit(solution)/shard_map/ppermute | solution.py:26
  85.3 77.7 %collective-permute-start.5 = (bf16[256,4096]{0,1:T(8,128)(2,1)S(1)}, bf16[256,4096]{0,1:T(8,128)(2,1)S(1)}, u32[]{:S(2)}, u32[]{:S(2)}) collective-permute-start(bf16[256,4096]{0,1:T(8,128)(2,1)S(1)} %maximum_select_fusion), channel_id=1, source_target_pairs={{0,2},{2,0},{4,6},{6,4},{8,10},{10,8},{12,14},{14,12},{16,18},{18,... | collective-permute-start | bytes 6291464 | tf_op jit(solution)/shard_map/ppermute | solution.py:16
  88.4 21.9 %collective-permute-start.8 = (f32[864,128]{1,0:T(8,128)S(1)}, f32[864,128]{1,0:T(8,128)S(1)}, u32[]{:S(2)}, u32[]{:S(2)}) collective-permute-start(f32[864,128]{1,0:T(8,128)S(1)} %constant_dynamic-slice_fusion.6), channel_id=1, source_target_pairs={{0,4},{2,6},{4,0},{6,2},{8,12},{10,14},{12,8},{14,10},{16,20},{18,... | collective-permute-start | bytes 1327112 | tf_op jit(solution)/shard_map/ppermute | solution.py:16
  90.0 33.3 %collective-permute-start.16 = (f32[864,128]{1,0:T(8,128)S(1)}, f32[864,128]{1,0:T(8,128)S(1)}, u32[]{:S(2)}, u32[]{:S(2)}) collective-permute-start(f32[864,128]{1,0:T(8,128)S(1)} %constant_dynamic-slice_fusion.2), channel_id=1, source_target_pairs={{0,8},{2,10},{4,12},{6,14},{8,0},{10,2},{12,4},{14,6},{16,24},{18,... | collective-permute-start | bytes 1327112 | tf_op jit(solution)/shard_map/ppermute | solution.py:16
  94.6 68.3 %collective-permute-start.4 = (bf16[128,4096]{0,1:T(8,128)(2,1)S(1)}, bf16[128,4096]{0,1:T(8,128)(2,1)S(1)}, u32[]{:S(2)}, u32[]{:S(2)}) collective-permute-start(bf16[128,4096]{0,1:T(8,128)(2,1)S(1)} %collective-permute-done.3), channel_id=1, source_target_pairs={{0,1},{1,0},{2,3},{3,2},{4,5},{5,4},{6,7},{7,6},{8,9},{9,8},{10,11... | collective-permute-start | bytes 3145736 | tf_op jit(solution)/shard_map/ppermute | solution.py:165
  110.4 22.2 %collective-permute-start.9 = (f32[432,128]{1,0:T(8,128)S(1)}, f32[432,128]{1,0:T(8,128)S(1)}, u32[]{:S(2)}, u32[]{:S(2)}) collective-permute-start(f32[432,128]{1,0:T(8,128)S(1)} %constant_dynamic-slice_fusion.5), channel_id=1, source_target_pairs={{0,8},{2,10},{4,12},{6,14},{8,0},{10,2},{12,4},{14,6},{16,24},{18,... | collective-permute-start | bytes 663560 | tf_op jit(solution)/shard_map/ppermute | solution.py:16
  123.4 14.4 %collective-permute-start.17 = (f32[432,128]{1,0:T(8,128)S(1)}, f32[432,128]{1,0:T(8,128)S(1)}, u32[]{:S(2)}, u32[]{:S(2)}) collective-permute-start(f32[432,128]{1,0:T(8,128)S(1)} %constant_dynamic-slice_fusion.1), channel_id=1, source_target_pairs={{0,16},{2,18},{4,20},{6,22},{8,24},{10,26},{12,28},{14,30},{16,0},... | collective-permute-start | bytes 663560 | tf_op jit(solution)/shard_map/ppermute | solution.py:16
  132.7 7.3 %collective-permute-start.10 = (f32[216,128]{1,0:T(8,128)S(1)}, f32[216,128]{1,0:T(8,128)S(1)}, u32[]{:S(2)}, u32[]{:S(2)}) collective-permute-start(f32[216,128]{1,0:T(8,128)S(1)} %constant_dynamic-slice_fusion.4), channel_id=1, source_target_pairs={{0,16},{2,18},{4,20},{6,22},{8,24},{10,26},{12,28},{14,30},{16,0},... | collective-permute-start | bytes 331784 | tf_op jit(solution)/shard_map/ppermute | solution.py:16
  137.9 5.4 %collective-permute-start.18 = (f32[216,128]{1,0:T(8,128)S(1)}, f32[216,128]{1,0:T(8,128)S(1)}, u32[]{:S(2)}, u32[]{:S(2)}) collective-permute-start(f32[216,128]{1,0:T(8,128)S(1)} %constant_dynamic-slice_fusion), channel_id=1, source_target_pairs={{0,4},{2,6},{4,0},{6,2},{8,12},{10,14},{12,8},{14,10},{16,20},{18,... | collective-permute-start | bytes 331784 | tf_op jit(solution)/shard_map/ppermute | solution.py:16
  140.0 8.2 %collective-permute-start.11 = (f32[216,128]{1,0:T(8,128)S(1)}, f32[216,128]{1,0:T(8,128)S(1)}, u32[]{:S(2)}, u32[]{:S(2)}) collective-permute-start(f32[216,128]{1,0:T(8,128)S(1)} %dynamic-slice_add_fusion.7), channel_id=1, source_target_pairs={{0,16},{2,18},{4,20},{6,22},{8,24},{10,26},{12,28},{14,30},{16,0},... | collective-permute-start | bytes 331784 | tf_op jit(solution)/shard_map/ppermute | solution.py:16
  143.3 5.0 %collective-permute-start.19 = (f32[216,128]{1,0:T(8,128)S(1)}, f32[216,128]{1,0:T(8,128)S(1)}, u32[]{:S(2)}, u32[]{:S(2)}) collective-permute-start(f32[216,128]{1,0:T(8,128)S(1)} %dynamic-slice_add_fusion.6), channel_id=1, source_target_pairs={{0,4},{2,6},{4,0},{6,2},{8,12},{10,14},{12,8},{14,10},{16,20},{18,... | collective-permute-start | bytes 331784 | tf_op jit(solution)/shard_map/ppermute | solution.py:16
  148.2 10.7 %collective-permute-start.12 = (f32[432,128]{1,0:T(8,128)S(1)}, f32[432,128]{1,0:T(8,128)S(1)}, u32[]{:S(2)}, u32[]{:S(2)}) collective-permute-start(f32[432,128]{1,0:T(8,128)S(1)} %pad_maximum_fusion.6), channel_id=1, source_target_pairs={{0,8},{2,10},{4,12},{6,14},{8,0},{10,2},{12,4},{14,6},{16,24},{18,... | collective-permute-start | bytes 663560 | tf_op jit(solution)/shard_map/ppermute | solution.py:16
  148.3 13.3 %copy-start.1 = (f32[256,4096]{1,0:T(8,128)S(1)}, f32[256,4096]{1,0:T(8,128)}, u32[]{:S(2)}) copy-start(f32[256,4096]{1,0:T(8,128)} %shard_map.59) | copy-start | bytes 12582916
  148.4 13.1 %collective-permute-start.20 = (f32[432,128]{1,0:T(8,128)S(1)}, f32[432,128]{1,0:T(8,128)S(1)}, u32[]{:S(2)}, u32[]{:S(2)}) collective-permute-start(f32[432,128]{1,0:T(8,128)S(1)} %pad_maximum_fusion.7), channel_id=1, source_target_pairs={{0,16},{2,18},{4,20},{6,22},{8,24},{10,26},{12,28},{14,30},{16,0},... | collective-permute-start | bytes 663560 | tf_op jit(solution)/shard_map/ppermute | solution.py:16
  159.0 17.1 %collective-permute-start.13 = (f32[864,128]{1,0:T(8,128)S(1)}, f32[864,128]{1,0:T(8,128)}, u32[]{:S(2)}, u32[]{:S(2)}) collective-permute-start(f32[864,128]{1,0:T(8,128)S(1)} %pad_maximum_fusion.4), channel_id=1, source_target_pairs={{0,4},{2,6},{4,0},{6,2},{8,12},{10,14},{12,8},{14,10},{16,20},{18,... | collective-permute-start | bytes 1327112 | tf_op jit(solution)/shard_map/ppermute | solution.py:16
  161.6 15.7 %collective-permute-start.21 = (f32[864,128]{1,0:T(8,128)S(1)}, f32[864,128]{1,0:T(8,128)}, u32[]{:S(2)}, u32[]{:S(2)}) collective-permute-start(f32[864,128]{1,0:T(8,128)S(1)} %pad_maximum_fusion.5), channel_id=1, source_target_pairs={{0,8},{2,10},{4,12},{6,14},{8,0},{10,2},{12,4},{14,6},{16,24},{18,... | collective-permute-start | bytes 1327112 | tf_op jit(solution)/shard_map/ppermute | solution.py:16
  177.2 30.8 %collective-permute-start.14 = (f32[1728,128]{1,0:T(8,128)S(1)}, f32[1728,128]{1,0:T(8,128)S(1)}, u32[]{:S(2)}, u32[]{:S(2)}) collective-permute-start(f32[1728,128]{1,0:T(8,128)S(1)} %pad_maximum_fusion.2), channel_id=1, source_target_pairs={{0,2},{2,0},{4,6},{6,4},{8,10},{10,8},{12,14},{14,12},{16,18},{18,... | collective-permute-start | bytes 2654216 | tf_op jit(solution)/shard_map/ppermute | solution.py:16
  178.5 29.7 %collective-permute-start.22 = (f32[1728,128]{1,0:T(8,128)S(1)}, f32[1728,128]{1,0:T(8,128)S(1)}, u32[]{:S(2)}, u32[]{:S(2)}) collective-permute-start(f32[1728,128]{1,0:T(8,128)S(1)} %pad_maximum_fusion.3), channel_id=1, source_target_pairs={{0,2},{2,0},{4,6},{6,4},{8,10},{10,8},{12,14},{14,12},{16,18},{18,... | collective-permute-start | bytes 2654216 | tf_op jit(solution)/shard_map/ppermute | solution.py:16
